TPU v7x, 128 devices: a whole 4x4x4 slice. The times are simulated.
128 devices in a mesh: scene: 8 (over y, core), frame: 16 (over z, x).
Axes of the slice: x: 4, y: 4, z: 4, core: 2. Of those that a mesh axis runs over, the one named last changes fastest.
Arguments:
- occupancy: bfloat16 [8, 64, 64, 2048], P('scene', 'frame'), may hold values from -6 to 6
- scene_lengths: int32 [8], P('scene'), may hold values from 8 to 64, as said below
- conv1_weight: bfloat16 [128, 1728], replicated, may hold values from -0.15625 to 0.15625
- conv2_weight: bfloat16 [256, 3456], replicated, may hold values from -0.109375 to 0.109375
- temporal_weight: bfloat16 [3, 256, 256], replicated, may hold values from -0.21875 to 0.21875
- query_weight: bfloat16 [256, 256], replicated
- key_weight: bfloat16 [256, 256], replicated
- value_weight: bfloat16 [256, 256], replicated, may hold values from -0.375 to 0.375
- out_weight: bfloat16 [256, 256], replicated, may hold values from -0.375 to 0.375
Outputs:
- encoded: bfloat16 [8, 64, 256, 512], P('scene', 'frame')
- kl_loss: float32 [], replicated
Inputs may be any that keep to these rules, and one draw needn't show every extreme that they name: `scene_lengths`: non-decreasing along the scenes; the first scene has exactly 8 frames with data and the last exactly 64.
All inputs are finite; a program needn't handle non-finite values.
Results may differ from a plain program's by a relative error of at most 0.011.
Values may be sent and summed in bfloat16 or wider, within the bound.
A program may use at most 192 MiB of HBM per device.

v0:
```python
import jax
import jax.numpy as jnp
from jax import lax
from jax.sharding import PartitionSpec as P

CIN = 64
C1 = 128
C2 = 256
HEADS = 4
HD = 64
HI = 16
ZD = 8
CELLS = 512
NORM_EPS = 1e-06


def extended(cells, sides, width):
    for axis, dim in sides:
        count = lax.axis_size(axis)
        ends = count - 1
        head = lax.slice_in_dim(cells, 0, width, axis=dim)
        tail = lax.slice_in_dim(cells, cells.shape[dim] - width, cells.shape[dim], axis=dim)
        cells = jnp.concatenate(
            [
                lax.ppermute(tail, axis, [(i, (i + 1) % count) for i in range(ends)]),
                cells,
                lax.ppermute(head, axis, [((i + 1) % count, i) for i in range(ends)]),
            ],
            axis=dim,
        )
    return cells


def spatial_conv(voxels, weight, channels_in, stride):
    channels_out = weight.shape[0]
    kernel = weight.reshape(channels_out, channels_in, 3, 3, 3)
    return lax.conv_general_dilated(
        voxels,
        kernel,
        (stride, stride, 1),
        ((1, 1), (1, 1), (1, 1)),
        dimension_numbers=("NCDHW", "OIDHW", "NCDHW"),
        preferred_element_type=jnp.float32,
    )


def mix_channels(weight, maps):
    return jnp.einsum("oc,fcn->fon", weight, maps, preferred_element_type=jnp.float32)


def temporal_block(padded, second_maps, temporal_weight):
    count_frames = second_maps.shape[0]
    temporal_sum = mix_channels(temporal_weight[0], padded[0:count_frames])
    for tap in range(1, 3):
        temporal_sum = temporal_sum + mix_channels(
            temporal_weight[tap], padded[tap : tap + count_frames]
        )
    residual_maps = (second_maps.astype(jnp.float32) + jax.nn.silu(temporal_sum)).astype(
        jnp.bfloat16
    )
    return residual_maps.astype(jnp.float32)


def project_rows(residual_f, query_weight, key_weight, value_weight):
    count_frames = residual_f.shape[0]
    count_cells = residual_f.shape[2]
    normed = (
        residual_f * lax.rsqrt(jnp.mean(residual_f * residual_f, axis=1, keepdims=True) + NORM_EPS)
    ).astype(jnp.bfloat16)
    queries = (
        mix_channels(query_weight, normed)
        .astype(jnp.bfloat16)
        .reshape(count_frames, HEADS, HD, count_cells)
    )
    key_rows = (
        mix_channels(key_weight, normed)
        .astype(jnp.bfloat16)
        .reshape(count_frames, HEADS, HD, count_cells)
    )
    value_rows = (
        mix_channels(value_weight, normed)
        .astype(jnp.bfloat16)
        .reshape(count_frames, HEADS, HD, count_cells)
    )
    return (queries, key_rows, value_rows)


def finish_rows(residual_f, attended, out_weight, valid_rows):
    count_frames = residual_f.shape[0]
    count_cells = residual_f.shape[2]
    out_full = residual_f + mix_channels(
        out_weight, attended.reshape(count_frames, C2, count_cells)
    )
    return (out_full * valid_rows[:, None, None]).astype(jnp.bfloat16)


def shards(
    occupancy,
    scene_lengths,
    conv1_weight,
    conv2_weight,
    temporal_weight,
    query_weight,
    key_weight,
    value_weight,
    out_weight,
):
    f_dev = occupancy.shape[1]
    length = scene_lengths[0]
    first_frame = lax.axis_index("frame") * f_dev
    frame_ids = first_frame + jnp.arange(f_dev, dtype=jnp.int32)
    valid_rows = (frame_ids < length).astype(jnp.float32)
    voxels = occupancy[0].reshape(f_dev, CIN, HI, HI, ZD)
    first_maps = jax.nn.silu(spatial_conv(voxels, conv1_weight, CIN, 2)).astype(jnp.bfloat16)
    second_full = jax.nn.silu(spatial_conv(first_maps, conv2_weight, C1, 1))
    second_maps = (second_full.reshape(f_dev, C2, CELLS) * valid_rows[:, None, None]).astype(
        jnp.bfloat16
    )
    padded = extended(second_maps, (("frame", 0),), 1)
    residual_f = temporal_block(padded, second_maps, temporal_weight)
    queries, key_rows, value_rows = project_rows(residual_f, query_weight, key_weight, value_weight)
    running_max = jnp.full((f_dev, HEADS, CELLS), -1e30, jnp.float32)
    panel_keys = lax.all_gather(key_rows, "frame", axis=0, tiled=True)
    panel_values = lax.all_gather(value_rows, "frame", axis=0, tiled=True)
    count_keys = panel_keys.shape[0]
    scores = jnp.einsum(
        "qhdc,khdc->qkhc", queries, panel_keys, preferred_element_type=jnp.float32
    ) * HD ** (-0.5)
    key_mask = (jnp.arange(count_keys) < length)[None, :, None, None]
    scores = jnp.where(key_mask, scores, -1e30)
    new_max = jnp.maximum(running_max, jnp.max(scores, axis=1))
    raw_weights = jnp.where(key_mask, jnp.exp(scores - new_max[:, None]), 0.0)
    new_sum = jnp.sum(raw_weights, axis=1)
    addition = jnp.einsum(
        "qkhc,khdc->qhdc",
        raw_weights.astype(jnp.bfloat16),
        panel_values,
        preferred_element_type=jnp.float32,
    )
    attended = (addition / new_sum[:, :, None, :]).astype(jnp.bfloat16)
    encoded = finish_rows(residual_f, attended, out_weight, valid_rows)
    squares = jnp.sum(jnp.square(encoded.astype(jnp.float32)))
    grand_total = lax.psum(squares, ("scene", "frame"))
    slot_count = float(lax.axis_size("scene") * lax.axis_size("frame") * f_dev * CELLS * C2)
    kl_loss = 0.5 * grand_total / slot_count
    return (encoded[None], kl_loss)


def solution(mesh):
    placed = (P("scene", "frame", None, None), P("scene"), P(), P(), P(), P(), P(), P(), P())
    return jax.shard_map(
        shards,
        mesh=mesh,
        in_specs=placed,
        out_specs=(P("scene", "frame", None, None), P()),
        check_vma=False,
    )
```

profile of v0, /device:TPU:1, one launch (start us, length us, event | category | flops | bytes accessed | tf_op | source)
XLA Modules:
  0.0 420.5 jit_solution(17460069256639030074)
XLA Ops:
  7.9 2.6 copy.62
  10.6 2.9 reshape.49
  14.5 1.5 reshape.48
  16.0 5.0 %fusion.28 = bf16[4,128,8,8,8]{1,0,4,3,2:T(4,128)(2,1)S(1)} fusion(bf16[4,64,16,16,8]{1,4,3,2,0:T(8,128)(2,1)S(1)} %bitcast.90, bf16[128,64,3,3,3]{0,4,3,2,1:T(4,128)(2,1)S(1)} %reshape.48), kind=kOutput, calls=%fused_computation.44 | convolution fusion | flops 764018688 | bytes 2015232 | tf_op jit(solution)/shard_map/conv_general_dilated | solution.py:37
  21.0 7.9 %multiply_convert_fusion = (bf16[4,256,8,8,8]{1,0,4,3,2:T(4,128)(2,1)S(1)}, f32[4,256,8,8,8]{1,0,4,3,2:T(4,128)}) fusion(f32[4]{0:T(128)S(1)} %compare_convert_fusion, bf16[4,128,8,8,8]{1,0,4,3,2:T(4,128)(2,1)S(1)} %fusion.28, bf16[256,128,3,3,3]{0,4,3,2,1:T(4,128)(2,1)S(1)} %copy-done.1), kind=kOutput, calls=%fused_computation.24 | convolution fusion | flops 2794455040 | bytes 5439504 | tf_op jit(solution)/shard_map/conv_general_dilated | solution.py:37
  28.9 1.9 copy.64
  31.2 4.0 collective-permute-start
  35.1 1.5 collective-permute-start.1
  37.1 3.0 collective-permute-done
  40.5 3.4 collective-permute-done.1
  45.0 1.4 convolution_convert_fusion.1
  46.5 1.4 convolution_convert_fusion.2
  48.4 2.5 copy.67
  50.9 112.4 %all-gather.5.cloned.1.call-done = bf16[64,4,64,512]{3,2,1,0:T(8,128)(2,1)} async-done(((bf16[4,4,64,512]{3,2,1,0:T(8,128)(2,1)}), bf16[64,4,64,512]{3,2,1,0:T(8,128)(2,1)}) %all-gather.5.cloned.1.call-update) | async-done | bytes 16777232 | tf_op jit(solution)/shard_map/all_gather | solution.py:123
  163.3 46.8 %copy.66 = bf16[64,4,64,512]{2,0,3,1:T(8,128)(2,1)} copy(bf16[64,4,64,512]{3,2,1,0:T(8,128)(2,1)} %all-gather.5.cloned.1.call-done) | data formatting | bytes 33554432 | tf_op jit(solution)/shard_map/all_gather | solution.py:123
  210.1 24.4 %bitcast_reduce_fusion = (f32[4,4,512]{0,2,1:T(8,128)}, f32[4,512,64,4]{2,3,1,0:T(4,128)}) fusion(pred[64]{0:T(512)(128)(4,1)S(1)} %iota_compare_fusion, bf16[64,4,64,512]{2,0,3,1:T(8,128)(2,1)} %copy.66, bf16[4,4,64,512]{2,0,3,1:T(4,128)(2,1)S(1)} %copy-done.2), kind=kOutput, calls=%fused_computation.1 | convolution fusion | flops 68673536 | bytes 19955776 | tf_op jit(solution)/shard_map/qhdc,khdc->qkhc/dot_general | solution.py:126
  234.5 1.4 broadcast_maximum_fusion
  235.9 30.0 %fusion.20 = f32[4,4,512]{0,2,1:T(8,128)S(1)} fusion(f32[4,4,512]{0,2,1:T(8,128)S(1)} %broadcast_maximum_fusion, f32[4,512,64,4]{2,3,1,0:T(4,128)} %get-tuple-element.9, pred[64]{0:T(512)(128)(4,1)S(1)} %iota_compare_fusion), kind=kLoop, calls=%fused_computation.34 | loop fusion | flops 2613248 | bytes 2162752 | tf_op jit(solution)/shard_map/reduce_sum | solution.py:133
  266.2 10.9 %all-gather.3.cloned.1.call-done = bf16[64,4,64,512]{3,2,1,0:T(8,128)(2,1)} async-done(((bf16[4,4,64,512]{3,2,1,0:T(8,128)(2,1)}), bf16[64,4,64,512]{3,2,1,0:T(8,128)(2,1)}) %all-gather.3.cloned.1.call-update) | async-done | bytes 16777232 | tf_op jit(solution)/shard_map/all_gather | solution.py:124
  277.1 46.6 %copy.68 = bf16[64,4,64,512]{2,0,3,1:T(8,128)(2,1)} copy(bf16[64,4,64,512]{3,2,1,0:T(8,128)(2,1)} %all-gather.3.cloned.1.call-done) | data formatting | bytes 33554432 | tf_op jit(solution)/shard_map/all_gather | solution.py:124
  323.7 17.5 %fusion.11 = f32[4,512,64,4]{2,3,1,0:T(4,128)} fusion(bf16[64,4,64,512]{2,0,3,1:T(8,128)(2,1)} %copy.68, f32[4,512,64,4]{2,3,1,0:T(4,128)} %get-tuple-element.9, f32[4,4,512]{0,2,1:T(8,128)S(1)} %broadcast_maximum_fusion, pred[64]{0:T(512)(128)(4,1)S(1)} %iota_compare_fusion), kind=kOutput, calls=%fused_computation.22 | convolution fusion | flops 69730304 | bytes 21004352 | tf_op jit(solution)/shard_map/qkhc,khdc->qhdc/dot_general | solution.py:134
  341.2 3.5 copy.69
  345.0 2.3 multiply_reduce_fusion
  347.3 64.6 %psum.7 = f32[]{:T(128)} all-reduce(f32[]{:T(128)} %get-tuple-element.10), channel_id=1, replica_groups=mesh['scene'=8,'frame'=16] {'scene','frame'}, use_global_device_ids=true, to_apply=%region_4.5 | all-reduce | flops 1 | bytes 8 | tf_op jit(solution)/shard_map/psum | solution.py:143
  (32 shorter events, 4.7 us)
Async XLA Ops:
  7.2 337.9 %copy-start = (bf16[256,256]{1,0:T(8,128)(2,1)S(1)}, bf16[256,256]{1,0:T(8,128)(2,1)}, u32[]{:S(2)}) copy-start(bf16[256,256]{1,0:T(8,128)(2,1)} %param.17) | copy-start | bytes 393220
  7.2 156.1 %all-gather.5.cloned.1.call-start = ((), (), s32[]{:S(2)}) async-start(), calls=%async_computation.1 | async-start | bytes 17825792 | tf_op jit(solution)/shard_map/all_gather | solution.py:123
  10.5 2.9 copy-start.3
  16.0 5.0 %copy-start.1 = (bf16[256,128,3,3,3]{0,4,3,2,1:T(4,128)(2,1)S(1)}, bf16[256,128,3,3,3]{0,4,3,2,1:T(4,128)(2,1)}, u32[]{:S(2)}) copy-start(bf16[256,128,3,3,3]{0,4,3,2,1:T(4,128)(2,1)} %reshape.49) | copy-start | bytes 5308420
  30.8 5.8 %copy-start.4 = (bf16[3,256,256]{2,1,0:T(8,128)(2,1)S(1)}, bf16[3,256,256]{2,1,0:T(8,128)(2,1)}, u32[]{:S(2)}) copy-start(bf16[3,256,256]{2,1,0:T(8,128)(2,1)} %param.13) | copy-start | bytes 1179652
  31.2 8.9 %collective-permute-start = (bf16[1,256,512]{2,1,0:T(8,128)(2,1)S(1)}, bf16[1,256,512]{2,1,0:T(8,128)(2,1)S(1)}, u32[]{:S(2)}, u32[]{:S(2)}) collective-permute-start(bf16[1,256,512]{2,1,0:T(8,128)(2,1)S(1)} %get-tuple-element.3), channel_id=1, source_target_pairs={{0,1},{1,2},{2,3},{3,4},{4,5},{5,6},{6,7},{7,8},{8,9},{9,10},{10,1... | collective-permute-start | bytes 786440 | tf_op jit(solution)/shard_map/ppermute | solution.py:25
  35.1 8.7 %collective-permute-start.1 = (bf16[1,256,512]{2,1,0:T(8,128)(2,1)S(1)}, bf16[1,256,512]{2,1,0:T(8,128)(2,1)S(1)}, u32[]{:S(2)}, u32[]{:S(2)}) collective-permute-start(bf16[1,256,512]{2,1,0:T(8,128)(2,1)S(1)} %get-tuple-element.2), channel_id=1, source_target_pairs={{1,0},{2,1},{3,2},{4,3},{5,4},{6,5},{7,6},{8,7},{9,8},{10,9},{11,1... | collective-permute-start | bytes 786440 | tf_op jit(solution)/shard_map/ppermute | solution.py:27
  40.5 4.5 %copy-start.5 = (bf16[256,256]{1,0:T(8,128)(2,1)S(1)}, bf16[256,256]{1,0:T(8,128)(2,1)}, u32[]{:S(2)}) copy-start(bf16[256,256]{1,0:T(8,128)(2,1)} %param.15) | copy-start | bytes 393220
  44.9 1.5 copy-start.6
  46.4 1.6 copy-start.7
  46.4 230.7 %all-gather.3.cloned.1.call-start = ((), (), s32[]{:S(2)}) async-start(), calls=%async_computation | async-start | bytes 17825792 | tf_op jit(solution)/shard_map/all_gather | solution.py:124
  50.9 159.2 %copy-start.2 = (bf16[4,4,64,512]{2,0,3,1:T(4,128)(2,1)S(1)}, bf16[4,4,64,512]{2,0,3,1:T(4,128)(2,1)}, u32[]{:S(2)}) copy-start(bf16[4,4,64,512]{2,0,3,1:T(4,128)(2,1)} %copy.67) | copy-start | bytes 3145732
Sparse Core Ops, SparseCore 0:
  46.6 116.7 all-gather.4
  166.0 111.0 all-gather.2
where the time goes:
time: 423 us; the launch traced here: 421 us
  waiting for transfers between devices  130 us (31%)
  local copies, waits for them, and re-layouts  110 us (26%)
  blocking collectives  64.6 us (15%)
  matrix products  62.2 us (15%)
  other arithmetic  32 us (8%)
  between operations  16.7 us (4%)
  starting transfers between devices  5.51 us (1%)
    all_gather x1, waiting for transfers between devices, shards(): panel_keys = lax.all_gather(key_rows, 'frame', axis=0, tiled=True)  112 us
    psum x1, blocking collectives, shards(): grand_total = lax.psum(squares, ('scene', 'frame'))  64.6 us
    all_gather x1, local copies, waits for them, and re-layouts, shards(): panel_keys = lax.all_gather(key_rows, 'frame', axis=0, tiled=True)  46.8 us
    all_gather x1, local copies, waits for them, and re-layouts, shards(): panel_values = lax.all_gather(value_rows, 'frame', axis=0, tiled=True)  46.6 us
    reduce_sum x1, other arithmetic, shards(): new_sum = jnp.sum(raw_weights, axis=1)  30 us
    dot_general x1, matrix products, shards(): jnp.einsum('qhdc,khdc->qkhc', queries, panel_keys, preferred_element_type...  24.4 us
    dot_general x1, matrix products, shards(): jnp.einsum('qkhc,khdc->qhdc', raw_weights.astype(jnp.bfloat16), panel_val...  17.5 us
    conv_general_dilated x2, matrix products, spatial_conv(): lax.conv_general_dilated(voxels, kernel, (stride, stride, 1), ((1, 1), (1...  12.8 us
  transfers between devices with their start and end apart: 4, of which 4 were waited for; matrix products, arithmetic and copies ran while one was open for 26% of the time, Pallas kernels for 0%

commit v1 on v0

--- a/solution.py
+++ b/solution.py
@@ -120,8 +120,13 @@
     residual_f = temporal_block(padded, second_maps, temporal_weight)
     queries, key_rows, value_rows = project_rows(residual_f, query_weight, key_weight, value_weight)
     running_max = jnp.full((f_dev, HEADS, CELLS), -1e30, jnp.float32)
-    panel_keys = lax.all_gather(key_rows, "frame", axis=0, tiled=True)
-    panel_values = lax.all_gather(value_rows, "frame", axis=0, tiled=True)
+
+    def write_object(view, mat):
+        finding = jnp.concatenate([view, mat], 1)
+        moved = lax.all_gather(finding, "frame", tiled=True, axis=0)
+        return jnp.split(moved, [view.shape[1]], 1)
+
+    panel_keys, panel_values = write_object(key_rows, value_rows)
     count_keys = panel_keys.shape[0]
     scores = jnp.einsum(
         "qhdc,khdc->qkhc", queries, panel_keys, preferred_element_type=jnp.float32

time: 423 us -> 523 us (1.24)
  waiting for transfers between devices: 130 us -> 205 us
  local copies, waits for them, and re-layouts: 110 us -> 134 us
    unnamed x18 -> x20, local copies, waits for them, and re-layouts: 3.74 us -> 98.5 us
    all_gather x2 -> x0, local copies, waits for them, and re-layouts: 93.4 us -> none  [the longest x1 46.8 us: shards(): panel_keys = lax.all_gather(key_rows, 'frame', axis=0, tiled=True)]
    all_gather x2 -> x1, waiting for transfers between devices: 123 us -> 199 us  [write_object(): moved = lax.all_gather(finding, 'frame', tiled=True, axis=0)]
    split x0 -> x1, local copies, waits for them, and re-layouts: none -> 23.2 us  [write_object(): return jnp.split(moved, [view.shape[1]], 1)]
  transfers between devices with their start and end apart: 4 -> 3, of which waited for: 4 -> 3; matrix products, arithmetic and copies ran while one was open for 26% -> 1% of each run, Pallas kernels for 0% -> 0%
where the time goes in v1:
time: 523 us; the launch traced here: 520 us
  waiting for transfers between devices  205 us (39%)
  local copies, waits for them, and re-layouts  134 us (26%)
  blocking collectives  64.6 us (12%)
  matrix products  60.2 us (12%)
  other arithmetic  33.5 us (6%)
  between operations  16.7 us (3%)
  starting transfers between devices  5.47 us (1%)
    all_gather x1, waiting for transfers between devices, write_object(): moved = lax.all_gather(finding, 'frame', tiled=True, axis=0)  199 us
    unnamed x20, local copies, waits for them, and re-layouts  98.5 us
    psum x1, blocking collectives, shards(): grand_total = lax.psum(squares, ('scene', 'frame'))  64.6 us
    reduce_sum x1, other arithmetic, shards(): new_sum = jnp.sum(raw_weights, axis=1)  30 us
    dot_general x1, matrix products, shards(): jnp.einsum('qhdc,khdc->qkhc', queries, panel_keys, preferred_element_type...  24.3 us
    split x1, local copies, waits for them, and re-layouts, write_object(): return jnp.split(moved, [view.shape[1]], 1)  23.2 us
    dot_general x1, matrix products, shards(): jnp.einsum('qkhc,khdc->qhdc', raw_weights.astype(jnp.bfloat16), panel_val...  17.5 us
    conv_general_dilated x2, matrix products, spatial_conv(): lax.conv_general_dilated(voxels, kernel, (stride, stride, 1), ((1, 1), (1...  12.8 us
  transfers between devices with their start and end apart: 3, of which 3 were waited for; matrix products, arithmetic and copies ran while one was open for 1% of the time, Pallas kernels for 0%

profile of v1, /device:TPU:1, one launch (start us, length us, event | category | flops | bytes accessed | tf_op | source)
XLA Modules:
  0.0 520.0 jit_solution(2546201668638889079)
XLA Ops:
  7.9 2.6 copy.62
  10.6 2.9 reshape.49
  13.4 1.1 copy.59
  14.5 1.5 reshape.48
  16.0 5.0 fusion.28
  21.0 7.8 %multiply_convert_fusion = (bf16[4,256,8,8,8]{1,0,4,3,2:T(4,128)(2,1)S(1)}, f32[4,256,8,8,8]{1,0,4,3,2:T(4,128)}) fusion(f32[4]{0:T(128)S(1)} %compare_convert_fusion, bf16[4,128,8,8,8]{1,0,4,3,2:T(4,128)(2,1)S(1)} %fusion.28, bf16[256,128,3,3,3]{0,4,3,2,1:T(4,128)(2,1)S(1)} %copy-done.1), kind=kOutput, calls=%fused_computation.25 | convolution fusion | flops 2794455040 | bytes 5439504 | tf_op jit(solution)/shard_map/conv_general_dilated | solution.py:37
  28.8 1.9 copy.64
  31.2 4.0 collective-permute-start
  35.1 1.5 collective-permute-start.1
  37.1 3.0 collective-permute-done
  40.5 3.4 collective-permute-done.1
  46.3 1.5 pad_maximum_fusion
  49.2 2.5 copy.68
  51.7 198.8 %all-gather.2.cloned.1.call-done = bf16[64,8,64,512]{3,2,1,0:T(8,128)(2,1)} async-done(((bf16[4,8,64,512]{3,2,1,0:T(8,128)(2,1)}), bf16[64,8,64,512]{3,2,1,0:T(8,128)(2,1)}) %all-gather.2.cloned.1.call-update) | async-done | bytes 33554448 | tf_op jit(solution)/shard_map/all_gather | solution.py:126
  250.5 23.2 %fusion.50 = (bf16[64,4,64,512]{3,2,1,0:T(8,128)(2,1)}, bf16[64,4,64,512]{3,2,1,0:T(8,128)(2,1)}) fusion(bf16[64,8,64,512]{3,2,1,0:T(8,128)(2,1)} %all-gather.2.cloned.1.call-done), kind=kLoop, calls=%fused_computation.66 | loop fusion | bytes 67108864 | tf_op jit(solution)/shard_map/split | solution.py:127
  273.7 46.8 %copy.76 = bf16[64,4,64,512]{2,0,3,1:T(8,128)(2,1)} copy(bf16[64,4,64,512]{3,2,1,0:T(8,128)(2,1)} %get-tuple-element.2) | data formatting | bytes 33554432
  320.5 24.3 %bitcast_reduce_fusion = (f32[4,4,512]{0,2,1:T(8,128)}, f32[4,512,64,4]{2,3,1,0:T(4,128)}) fusion(pred[64]{0:T(512)(128)(4,1)S(1)} %iota_compare_fusion, bf16[64,4,64,512]{2,0,3,1:T(8,128)(2,1)} %copy.76, bf16[4,4,64,512]{2,0,3,1:T(4,128)(2,1)S(1)} %copy-done.2), kind=kOutput, calls=%fused_computation.1 | convolution fusion | flops 68673536 | bytes 19955776 | tf_op jit(solution)/shard_map/qhdc,khdc->qkhc/dot_general | solution.py:131
  344.9 1.3 broadcast_maximum_fusion
  346.2 30.0 %fusion.20 = f32[4,4,512]{0,2,1:T(8,128)S(1)} fusion(f32[4,4,512]{0,2,1:T(8,128)S(1)} %broadcast_maximum_fusion, f32[4,512,64,4]{2,3,1,0:T(4,128)} %get-tuple-element.11, pred[64]{0:T(512)(128)(4,1)S(1)} %iota_compare_fusion), kind=kLoop, calls=%fused_computation.35 | loop fusion | flops 2613248 | bytes 2162752 | tf_op jit(solution)/shard_map/reduce_sum | solution.py:138
  376.5 46.7 %copy.75 = bf16[64,4,64,512]{2,0,3,1:T(8,128)(2,1)} copy(bf16[64,4,64,512]{3,2,1,0:T(8,128)(2,1)} %get-tuple-element.3) | data formatting | bytes 33554432
  423.2 17.5 %fusion.11 = f32[4,512,64,4]{2,3,1,0:T(4,128)} fusion(bf16[64,4,64,512]{2,0,3,1:T(8,128)(2,1)} %copy.75, f32[4,512,64,4]{2,3,1,0:T(4,128)} %get-tuple-element.11, f32[4,4,512]{0,2,1:T(8,128)S(1)} %broadcast_maximum_fusion, pred[64]{0:T(512)(128)(4,1)S(1)} %iota_compare_fusion), kind=kOutput, calls=%fused_computation.23 | convolution fusion | flops 69730304 | bytes 21004352 | tf_op jit(solution)/shard_map/qkhc,khdc->qhdc/dot_general | solution.py:139
  440.6 3.5 copy.69
  444.5 2.3 multiply_reduce_fusion
  446.7 64.6 %psum.7 = f32[]{:T(128)} all-reduce(f32[]{:T(128)} %get-tuple-element.12), channel_id=1, replica_groups=mesh['scene'=8,'frame'=16] {'scene','frame'}, use_global_device_ids=true, to_apply=%region_4.5 | all-reduce | flops 1 | bytes 8 | tf_op jit(solution)/shard_map/psum | solution.py:148
  (31 shorter events, 5.7 us)
Async XLA Ops:
  7.2 437.3 %copy-start = (bf16[256,256]{1,0:T(8,128)(2,1)S(1)}, bf16[256,256]{1,0:T(8,128)(2,1)}, u32[]{:S(2)}) copy-start(bf16[256,256]{1,0:T(8,128)(2,1)} %param.17) | copy-start | bytes 393220
  7.2 243.3 %all-gather.2.cloned.1.call-start = ((), (), s32[]{:S(2)}) async-start(), calls=%async_computation | async-start | bytes 35651584 | tf_op jit(solution)/shard_map/all_gather | solution.py:126
  10.5 2.9 copy-start.3
  16.0 5.0 copy-start.1
  30.8 5.8 %copy-start.4 = (bf16[3,256,256]{2,1,0:T(8,128)(2,1)S(1)}, bf16[3,256,256]{2,1,0:T(8,128)(2,1)}, u32[]{:S(2)}) copy-start(bf16[3,256,256]{2,1,0:T(8,128)(2,1)} %param.13) | copy-start | bytes 1179652
  31.2 8.9 %collective-permute-start = (bf16[1,256,512]{2,1,0:T(8,128)(2,1)S(1)}, bf16[1,256,512]{2,1,0:T(8,128)(2,1)S(1)}, u32[]{:S(2)}, u32[]{:S(2)}) collective-permute-start(bf16[1,256,512]{2,1,0:T(8,128)(2,1)S(1)} %get-tuple-element.5), channel_id=1, source_target_pairs={{0,1},{1,2},{2,3},{3,4},{4,5},{5,6},{6,7},{7,8},{8,9},{9,10},{10,1... | collective-permute-start | bytes 786440 | tf_op jit(solution)/shard_map/ppermute | solution.py:25
  35.1 8.8 %collective-permute-start.1 = (bf16[1,256,512]{2,1,0:T(8,128)(2,1)S(1)}, bf16[1,256,512]{2,1,0:T(8,128)(2,1)S(1)}, u32[]{:S(2)}, u32[]{:S(2)}) collective-permute-start(bf16[1,256,512]{2,1,0:T(8,128)(2,1)S(1)} %get-tuple-element.4), channel_id=1, source_target_pairs={{1,0},{2,1},{3,2},{4,3},{5,4},{6,5},{7,6},{8,7},{9,8},{10,9},{11,1... | collective-permute-start | bytes 786440 | tf_op jit(solution)/shard_map/ppermute | solution.py:27
  40.5 4.5 copy-start.5
  44.9 0.9 copy-start.6
  47.8 0.9 copy-start.7
  273.7 46.8 %copy-start.2 = (bf16[4,4,64,512]{2,0,3,1:T(4,128)(2,1)S(1)}, bf16[4,4,64,512]{2,0,3,1:T(4,128)(2,1)}, u32[]{:S(2)}) copy-start(bf16[4,4,64,512]{2,0,3,1:T(4,128)(2,1)} %copy.68) | copy-start | bytes 3145732
Sparse Core Ops, SparseCore 0:
  48.0 202.4 all-gather.1
